TPU v7x, 32 devices: a whole 2x2x4 slice. The times are simulated.
32 devices in a mesh: dom: 8 (over z, y), feat: 4 (over x, core).
Axes of the slice: x: 2, y: 2, z: 4, core: 2. Of those that a mesh axis runs over, the one named last changes fastest.
Arguments:
- features: bfloat16 [32768, 512], P('dom', 'feat'), may hold values from -6 to 6
- theta: bfloat16 [512, 512], P(None, 'feat'), may hold values from -0.25 to 0.25
- incidence: int32 [3, 4096], P(None, 'dom'), may hold values from 0 to 4095, as said below
- edge_weight: float32 [16384], P('dom'), may hold values from 0.5 to 2
- cotangent: bfloat16 [32768, 512], P('dom', 'feat'), may hold values from -6 to 6
Outputs:
- activation: bfloat16 [32768, 512], P('dom', 'feat')
- grad_features: bfloat16 [32768, 512], P('dom', 'feat')
- grad_theta: float32 [512, 512], P('dom', 'feat')
Inputs may be any that keep to these rules, and one draw needn't show every extreme that they name: `incidence`: in the 64 slots from one vertex owner to one hyperedge owner the live slots (weight over zero) come first, at least one of them; some hyperedge owner receives all 64 slots live from every vertex owner.
All inputs are finite; a program needn't handle non-finite values.
Results may differ from a plain program's by a relative error of at most 0.0073.
Values may be sent and summed in bfloat16 or wider, within the bound.
A program may use at most 64 MiB of HBM per device.

v0:
```python
import jax
import jax.numpy as jnp
from jax import lax
from jax.sharding import PartitionSpec as P


def local(features, theta, incidence, edge_weight, cotangent):
    owners = lax.axis_size("dom")
    nvert = features.shape[0]
    cols = features.shape[1]
    nedge = edge_weight.shape[0]
    vert = incidence[0]
    edge = incidence[1]
    weight = incidence[2]
    weight_f = weight.astype(jnp.float32)
    dvis = lax.rsqrt(1.0 + jax.ops.segment_sum(weight_f, vert, num_segments=nvert))
    slot_scale = weight_f * dvis[vert]
    full_rows = lax.all_gather(features, "feat", axis=1, tiled=True)
    projected = jnp.dot(full_rows, theta, preferred_element_type=jnp.float32).astype(jnp.bfloat16)
    message = (slot_scale[:, None] * projected[vert].astype(jnp.float32)).astype(jnp.bfloat16)
    recv_rows, recv_edge, recv_weight = (
        lax.all_to_all(
            message.reshape(owners, -1, cols), "dom", split_axis=0, concat_axis=0, tiled=True
        ),
        lax.all_to_all(edge.reshape(owners, -1), "dom", split_axis=0, concat_axis=0, tiled=True),
        lax.all_to_all(weight.reshape(owners, -1), "dom", split_axis=0, concat_axis=0, tiled=True),
    )
    recv_edge = recv_edge.reshape(-1)
    degree = 1.0 + jax.ops.segment_sum(
        recv_weight.reshape(-1).astype(jnp.float32), recv_edge, num_segments=nedge
    )
    edge_scale = edge_weight / degree

    def edge_side(rows):
        edge_sum = jax.ops.segment_sum(
            rows.reshape(-1, cols).astype(jnp.float32), recv_edge, num_segments=nedge
        )
        edge_rows = (edge_scale[:, None] * edge_sum).astype(jnp.bfloat16)
        return edge_rows[recv_edge].reshape(owners, -1, cols)

    def vertex_side(back):
        terms = weight_f[:, None] * back.reshape(-1, cols).astype(jnp.float32)
        return dvis[:, None] * jax.ops.segment_sum(terms, vert, num_segments=nvert)

    back = lax.all_to_all(edge_side(recv_rows), "dom", split_axis=0, concat_axis=0, tiled=True)
    summed = vertex_side(back)
    sigma = jax.nn.sigmoid(summed)
    activation = (summed * sigma).astype(jnp.bfloat16)
    slope = sigma * (1.0 + summed * (1.0 - sigma))
    grad_summed = cotangent.astype(jnp.float32) * slope
    grad_message = (slot_scale[:, None] * grad_summed[vert]).astype(jnp.bfloat16)
    grad_recv = lax.all_to_all(
        grad_message.reshape(owners, -1, cols), "dom", split_axis=0, concat_axis=0, tiled=True
    )
    grad_back = lax.all_to_all(edge_side(grad_recv), "dom", split_axis=0, concat_axis=0, tiled=True)
    grad_projected = vertex_side(grad_back).astype(jnp.bfloat16)
    theta_full = lax.all_gather(theta, "feat", axis=1, tiled=True)
    theta_mine = lax.dynamic_slice_in_dim(theta_full, lax.axis_index("feat") * cols, cols, 0)
    grad_total = lax.dot_general(
        lax.all_gather(grad_projected, "feat", axis=1, tiled=True),
        theta_mine,
        (((1,), (1,)), ((), ())),
        preferred_element_type=jnp.float32,
    )
    grad_features = grad_total.astype(jnp.bfloat16)
    share = full_rows.shape[1] // owners
    term = lax.dot_general(
        full_rows, grad_projected, (((0,), (0,)), ((), ())), preferred_element_type=jnp.float32
    )
    total = lax.psum(term, "dom")
    grad_theta = lax.dynamic_slice_in_dim(total, lax.axis_index("dom") * share, share, 0)
    return (activation, grad_features, grad_theta)


def solution(mesh):
    placed = (P("dom", "feat"), P(None, "feat"), P(None, "dom"), P("dom"), P("dom", "feat"))
    return jax.shard_map(
        local,
        mesh=mesh,
        in_specs=placed,
        out_specs=(P("dom", "feat"), P("dom", "feat"), P("dom", "feat")),
        check_vma=False,
    )
```

profile of v0, /device:TPU:0, one launch (start us, length us, event | category | flops | bytes accessed | tf_op | source)
XLA Modules:
  0.0 234.5 jit_solution(12169646869658793668)
XLA Ops:
  9.4 7.3 %all-to-all-start = ((s32[8,1,64]{2,1,0:T(1,128)}), s32[8,1,64]{2,1,0:T(1,128)S(1)}, u32[]{:S(2)}, u32[]{:S(2)}) async-start(s32[8,1,64]{2,1,0:T(1,128)} %all_to_all.24), calls=%async_computation | async-start | bytes 8192 | tf_op jit(solution)/shard_map/all_to_all | solution.py:25
  18.8 4.3 %all-to-all-done = s32[8,1,64]{2,1,0:T(1,128)S(1)} async-done(((s32[8,1,64]{2,1,0:T(1,128)}), s32[8,1,64]{2,1,0:T(1,128)S(1)}, u32[]{:S(2)}, u32[]{:S(2)}) %all-to-all-start) | async-done | bytes 2080 | tf_op jit(solution)/shard_map/all_to_all | solution.py:25
  23.1 3.3 %all-to-all-start.1 = ((s32[8,1,64]{2,1,0:T(1,128)}), s32[8,1,64]{2,1,0:T(1,128)S(1)}, u32[]{:S(2)}, u32[]{:S(2)}) async-start(s32[8,1,64]{2,1,0:T(1,128)} %all_to_all.26), calls=%async_computation.1 | async-start | bytes 8192 | tf_op jit(solution)/shard_map/all_to_all | solution.py:26
  26.5 3.3 %scatter_custom_fusion = f32[4096]{0:T(1024)S(1)} fusion(s32[512]{0:T(512)S(1)} %bitcast.41, f32[512]{0:T(512)S(1)} %bitcast.36, f32[]{:T(128)} %constant.11.clone.1), kind=kCustom, calls=%fused_computation.40 | custom fusion | flops 512 | bytes 16388 | tf_op jit(solution)/shard_map/scatter-add | solution.py:16
  29.8 3.1 %gather_fusion = f32[512]{0:T(512)S(1)} fusion(f32[4096]{0:T(1024)S(1)} %rsqrt.3, s32[1024]{0:T(1024)S(1)} %pad_clamp_fusion.1), kind=kCustom, calls=%fused_computation | custom fusion | bytes 6144 | tf_op jit(solution)/shard_map/gather | solution.py:17
  34.4 3.3 %scatter_custom_fusion.1 = f32[2048]{0:T(1024)S(1)} fusion(s32[512]{0:T(512)S(1)} %reshape.181, f32[512]{0:T(512)S(1)} %reshape.183, f32[]{:T(128)} %constant.11.clone.1), kind=kCustom, calls=%fused_computation.45 | custom fusion | flops 512 | bytes 8196 | tf_op jit(solution)/shard_map/scatter-add | solution.py:29
  37.7 9.6 %all-gather.3.cloned.1.call-done = bf16[4096,512]{1,0:T(8,128)(2,1)} async-done(((bf16[4096,128]{1,0:T(8,128)(2,1)}), bf16[4096,512]{1,0:T(8,128)(2,1)}) %all-gather.3.cloned.1.call-update) | async-done | bytes 4194320 | tf_op jit(solution)/shard_map/all_gather | solution.py:18
  47.3 3.4 %convolution_convert_fusion.1 = bf16[4096,128]{1,0:T(8,128)(2,1)S(1)} fusion(bf16[4096,512]{1,0:T(8,128)(2,1)} %all-gather.3.cloned.1.call-done, bf16[512,128]{1,0:T(8,128)(2,1)S(1)} %copy-done.2), kind=kOutput, calls=%fused_computation.12 | convolution fusion | flops 537395200 | bytes 5373952 | tf_op jit(solution)/shard_map/dot_general | solution.py:19
  52.9 5.5 %all-to-all-start.2 = ((bf16[8,64,128]{2,1,0:T(8,128)(2,1)}), bf16[8,64,128]{2,1,0:T(8,128)(2,1)S(1)}, u32[]{:S(2)}, u32[]{:S(2)}) async-start(bf16[8,64,128]{2,1,0:T(8,128)(2,1)} %fusion.10), calls=%async_computation.2 | async-start | bytes 262144 | tf_op jit(solution)/shard_map/all_to_all | solution.py:22
  58.5 7.3 %all-to-all-done.2 = bf16[8,64,128]{2,1,0:T(8,128)(2,1)S(1)} async-done(((bf16[8,64,128]{2,1,0:T(8,128)(2,1)}), bf16[8,64,128]{2,1,0:T(8,128)(2,1)S(1)}, u32[]{:S(2)}, u32[]{:S(2)}) %all-to-all-start.2) | async-done | bytes 131104 | tf_op jit(solution)/shard_map/all_to_all | solution.py:22
  65.8 2.5 %scatter_custom_fusion.2 = f32[2048,128]{1,0:T(8,128)S(1)} fusion(s32[512]{0:T(512)S(1)} %reshape.181, f32[]{:T(128)} %constant.12.clone.1, bf16[512,128]{1,0:T(8,128)(2,1)S(1)} %bitcast.28), kind=kCustom, calls=%fused_computation.26 | custom fusion | flops 131072 | bytes 1179652 | tf_op jit(solution)/shard_map/scatter-add | solution.py:35
  68.7 1.3 gather_fusion.2
  70.1 9.9 %all_to_all.38 = bf16[8,64,128]{2,1,0:T(8,128)(2,1)S(1)} all-to-all(bf16[8,64,128]{2,1,0:T(8,128)(2,1)S(1)} %bitcast.33), channel_id=1, replica_groups=mesh['dom'=8,'feat'=4] {'dom'}, dimensions={0} | all-to-all | bytes 262144 | tf_op jit(solution)/shard_map/all_to_all | solution.py:45
  79.9 3.8 %scatter_custom_fusion.3 = f32[4096,128]{1,0:T(8,128)} fusion(s32[512]{0:T(512)S(1)} %bitcast.42, f32[]{:T(128)} %constant.12.clone.1, bf16[512,128]{1,0:T(8,128)(2,1)S(1)} %bitcast.34, f32[512]{0:T(512)S(1)} %bitcast.37), kind=kCustom, calls=%fused_computation.22 | custom fusion | flops 196608 | bytes 2230276 | tf_op jit(solution)/shard_map/scatter-add | solution.py:43
  83.7 3.2 %multiply_multiply_fusion = (f32[4096,128]{1,0:T(8,128)S(1)}, bf16[4096,128]{1,0:T(8,128)(2,1)}) fusion(bf16[4096,128]{1,0:T(8,128)(2,1)S(1)} %copy-done.1, f32[4096,128]{1,0:T(8,128)} %scatter_custom_fusion.3, f32[4096]{0:T(1024)S(1)} %rsqrt.3), kind=kLoop, calls=%fused_computation.14 | loop fusion | flops 6291456 | bytes 6307840 | tf_op jit(solution)/shard_map/mul | solution.py:50
  88.1 9.7 %all_to_all.39 = bf16[8,64,128]{2,1,0:T(8,128)(2,1)S(1)} all-to-all(bf16[8,64,128]{2,1,0:T(8,128)(2,1)S(1)} %multiply_convert_fusion.4), channel_id=1, replica_groups=mesh['dom'=8,'feat'=4] {'dom'}, dimensions={0} | all-to-all | bytes 262144 | tf_op jit(solution)/shard_map/all_to_all | solution.py:52
  97.8 2.5 %scatter_custom_fusion.4 = f32[2048,128]{1,0:T(8,128)S(1)} fusion(s32[512]{0:T(512)S(1)} %reshape.181, f32[]{:T(128)} %constant.12.clone.1, bf16[512,128]{1,0:T(8,128)(2,1)S(1)} %bitcast.30), kind=kCustom, calls=%fused_computation.24 | custom fusion | flops 131072 | bytes 1179652 | tf_op jit(solution)/shard_map/scatter-add | solution.py:35
  102.0 9.7 %all_to_all.40 = bf16[8,64,128]{2,1,0:T(8,128)(2,1)S(1)} all-to-all(bf16[8,64,128]{2,1,0:T(8,128)(2,1)S(1)} %bitcast.31), channel_id=1, replica_groups=mesh['dom'=8,'feat'=4] {'dom'}, dimensions={0} | all-to-all | bytes 262144 | tf_op jit(solution)/shard_map/all_to_all | solution.py:55
  111.7 2.9 %scatter_custom_fusion.5 = f32[4096,128]{1,0:T(8,128)S(1)} fusion(s32[512]{0:T(512)S(1)} %bitcast.43, f32[]{:T(128)} %constant.12.clone.1, bf16[512,128]{1,0:T(8,128)(2,1)S(1)} %bitcast.29, f32[512]{0:T(512)S(1)} %bitcast.38), kind=kCustom, calls=%fused_computation.20 | custom fusion | flops 196608 | bytes 2230276 | tf_op jit(solution)/shard_map/scatter-add | solution.py:43
  115.4 4.0 %convolution_bitcast_fusion = f32[512,128]{0,1:T(8,128)} fusion(bf16[4096,128]{1,0:T(8,128)(2,1)S(1)} %multiply_convert_fusion, bf16[4096,512]{1,0:T(8,128)(2,1)} %all-gather.3.cloned.1.call-done), kind=kOutput, calls=%fused_computation.17 | convolution fusion | flops 536870912 | bytes 5505024 | tf_op jit(solution)/shard_map/dot_general | solution.py:67
  120.2 6.5 %all_gather.11 = bf16[512,512]{1,0:T(8,128)(2,1)S(1)} all-gather(bf16[512,128]{1,0:T(8,128)(2,1)S(1)} %copy-done.2), channel_id=1, replica_groups=mesh['dom'=8,'feat'=4] {'feat'}, dimensions={1}, use_global_device_ids=true | all-gather | bytes 655360 | tf_op jit(solution)/shard_map/all_gather | solution.py:57
  126.7 60.2 %all-reduce.2.cloned.1.call-done = f32[512,128]{0,1:T(8,128)} async-done(((f32[512,128]{0,1:T(8,128)}), f32[512,128]{0,1:T(8,128)}) %all-reduce.2.cloned.1.call-update) | async-done | bytes 262160 | tf_op jit(solution)/shard_map/psum | solution.py:70
  188.6 34.9 %all-gather.5.cloned.1.call-done = bf16[4096,512]{1,0:T(8,128)(2,1)} async-done(((bf16[4096,128]{1,0:T(8,128)(2,1)}), bf16[4096,512]{1,0:T(8,128)(2,1)}) %all-gather.5.cloned.1.call-update) | async-done | bytes 4194320 | tf_op jit(solution)/shard_map/all_gather | solution.py:60
  223.5 4.4 %convolution_convert_fusion = bf16[4096,128]{1,0:T(8,128)(2,1)} fusion(bf16[4096,512]{1,0:T(8,128)(2,1)} %all-gather.5.cloned.1.call-done, bf16[512,512]{1,0:T(8,128)(2,1)S(1)} %all_gather.11, s32[]{:T(128)S(6)} %select_n.31), kind=kOutput, calls=%fused_computation.11 | convolution fusion | flops 537395200 | bytes 5373956 | tf_op jit(solution)/shard_map/dot_general | solution.py:59
  (44 shorter events, 14.4 us)
Async XLA Ops:
  7.2 30.6 %copy-start.3 = (f32[2048]{0:T(1024)S(1)}, f32[2048]{0:T(1024)}, u32[]{:S(2)}) copy-start(f32[2048]{0:T(1024)} %param.8) | copy-start | bytes 24580
  7.2 40.2 %copy-start.2 = (bf16[512,128]{1,0:T(8,128)(2,1)S(1)}, bf16[512,128]{1,0:T(8,128)(2,1)}, u32[]{:S(2)}) copy-start(bf16[512,128]{1,0:T(8,128)(2,1)} %param.6) | copy-start | bytes 393220
  7.2 40.1 %all-gather.3.cloned.1.call-start = ((), (), s32[]{:S(2)}) async-start(), calls=%async_computation.6 | async-start | bytes 5242880 | tf_op jit(solution)/shard_map/all_gather | solution.py:18
  9.4 13.7 %all-to-all-start = ((s32[8,1,64]{2,1,0:T(1,128)}), s32[8,1,64]{2,1,0:T(1,128)S(1)}, u32[]{:S(2)}, u32[]{:S(2)}) async-start(s32[8,1,64]{2,1,0:T(1,128)} %all_to_all.24), calls=%async_computation | async-start | bytes 8192 | tf_op jit(solution)/shard_map/all_to_all | solution.py:25
  23.1 11.3 %all-to-all-start.1 = ((s32[8,1,64]{2,1,0:T(1,128)}), s32[8,1,64]{2,1,0:T(1,128)S(1)}, u32[]{:S(2)}, u32[]{:S(2)}) async-start(s32[8,1,64]{2,1,0:T(1,128)} %all_to_all.26), calls=%async_computation.1 | async-start | bytes 8192 | tf_op jit(solution)/shard_map/all_to_all | solution.py:26
  52.9 12.9 %all-to-all-start.2 = ((bf16[8,64,128]{2,1,0:T(8,128)(2,1)}), bf16[8,64,128]{2,1,0:T(8,128)(2,1)S(1)}, u32[]{:S(2)}, u32[]{:S(2)}) async-start(bf16[8,64,128]{2,1,0:T(8,128)(2,1)} %fusion.10), calls=%async_computation.2 | async-start | bytes 262144 | tf_op jit(solution)/shard_map/all_to_all | solution.py:22
  58.4 128.5 %all-reduce.2.cloned.1.call-start = ((), (), s32[]{:S(2)}) async-start(), calls=%async_computation.8 | async-start | bytes 524288 | tf_op jit(solution)/shard_map/psum | solution.py:70
  68.7 15.0 %copy-start.1 = (bf16[4096,128]{1,0:T(8,128)(2,1)S(1)}, bf16[4096,128]{1,0:T(8,128)(2,1)}, u32[]{:S(2)}) copy-start(bf16[4096,128]{1,0:T(8,128)(2,1)} %param.9) | copy-start | bytes 3145732
  115.4 4.1 %copy-start = (bf16[4096,128]{1,0:T(8,128)(2,1)}, bf16[4096,128]{1,0:T(8,128)(2,1)S(1)}, u32[]{:S(2)}) copy-start(bf16[4096,128]{1,0:T(8,128)(2,1)S(1)} %multiply_convert_fusion) | copy-start | bytes 3145732
  119.4 104.1 %all-gather.5.cloned.1.call-start = ((), (), s32[]{:S(2)}) async-start(), calls=%async_computation.7 | async-start | bytes 5242880 | tf_op jit(solution)/shard_map/all_gather | solution.py:60
Sparse Core Ops, SparseCore 0:
  9.6 37.7 all-gather.2
  119.6 67.3 all-reduce.1
  189.2 34.2 all-gather.4
where the time goes:
time: 235 us; the launch traced here: 234 us
  waiting for transfers between devices  118 us (50%)
  blocking collectives  35.9 us (15%)
  other arithmetic  26.6 us (11%)
  starting transfers between devices  16.2 us (7%)
  between operations  14 us (6%)
  local copies, waits for them, and re-layouts  12.1 us (5%)
  matrix products  11.9 us (5%)
    psum x1, waiting for transfers between devices, local(): total = lax.psum(term, 'dom')  60.2 us
    all_gather x1, waiting for transfers between devices, local(): lax.all_gather(grad_projected, 'feat', axis=1, tiled=True)  34.9 us
    all_to_all x1, blocking collectives, local(): lax.all_to_all(edge_side(recv_rows), 'dom', split_axis=0, concat_axis=0,...  9.85 us
    all_to_all x1, blocking collectives, local(): lax.all_to_all(grad_message.reshape(owners, -1, cols), 'dom', split_axis=...  9.74 us
    all_to_all x1, blocking collectives, local(): lax.all_to_all(edge_side(grad_recv), 'dom', split_axis=0, concat_axis=0,...  9.74 us
    all_gather x1, waiting for transfers between devices, local(): full_rows = lax.all_gather(features, 'feat', axis=1, tiled=True)  9.59 us
    all_to_all x1, waiting for transfers between devices, local(): lax.all_to_all(message.reshape(owners, -1, cols), 'dom', split_axis=0, co...  7.34 us
    all_to_all x1, starting transfers between devices, local(): lax.all_to_all(edge.reshape(owners, -1), 'dom', split_axis=0, concat_axis...  7.28 us
  transfers between devices with their start and end apart: 6, of which 5 were waited for; matrix products, arithmetic and copies ran while one was open for 6% of the time, Pallas kernels for 0%

commit v1 on v0

--- a/solution.py
+++ b/solution.py
@@ -5,6 +5,19 @@
 
 
 def local(features, theta, incidence, edge_weight, cotangent):
+
+    def resolve_block(content, mesh_dim, d0):
+        axis_total = jax.lax.axis_size(mesh_dim)
+        new = [(rr - 1, rr) for rr in range(1, axis_total)] + [(axis_total - 1, 0)]
+        local_next = content
+        tray = [local_next]
+        for _ in range(axis_total - 1):
+            local_next = jax.lax.ppermute(local_next, mesh_dim, perm=new)
+            tray += [local_next]
+        base_arr = jnp.concatenate([*reversed(tray)], axis=d0)
+        even = jax.lax.axis_index(mesh_dim)
+        return jnp.roll(base_arr, (even + 1) * local_next.shape[d0], axis=d0)
+
     owners = lax.axis_size("dom")
     nvert = features.shape[0]
     cols = features.shape[1]
@@ -15,7 +28,7 @@
     weight_f = weight.astype(jnp.float32)
     dvis = lax.rsqrt(1.0 + jax.ops.segment_sum(weight_f, vert, num_segments=nvert))
     slot_scale = weight_f * dvis[vert]
-    full_rows = lax.all_gather(features, "feat", axis=1, tiled=True)
+    full_rows = resolve_block(features, "feat", 1)
     projected = jnp.dot(full_rows, theta, preferred_element_type=jnp.float32).astype(jnp.bfloat16)
     message = (slot_scale[:, None] * projected[vert].astype(jnp.float32)).astype(jnp.bfloat16)
     recv_rows, recv_edge, recv_weight = (

time: 235 us -> 223 us (0.949)
  waiting for transfers between devices: 118 us -> 93.9 us
  local copies, waits for them, and re-layouts: 12.1 us -> 20.4 us
    all_gather x1, waiting for transfers between devices: 34.9 us -> 0.01 us  [local(): lax.all_gather(grad_projected, 'feat', axis=1, tiled=True)]
    ppermute x0 -> x3, waiting for transfers between devices: none -> 28.8 us  [resolve_block(): local_next = jax.lax.ppermute(local_next, mesh_dim, perm=new)]
    all_gather x1 -> x0, waiting for transfers between devices: 9.59 us -> none  [local(): full_rows = lax.all_gather(features, 'feat', axis=1, tiled=True)]
    unnamed x9 -> x19, local copies, waits for them, and re-layouts: 0.73 us -> 8.2 us
    all_to_all x1, waiting for transfers between devices: 7.34 us -> 2.94 us  [local(): lax.all_to_all(message.reshape(owners, -1, cols), 'dom', split_axis=0, co...]
    all_to_all x1, waiting for transfers between devices: 4.3 us -> 0.93 us  [local(): lax.all_to_all(edge.reshape(owners, -1), 'dom', split_axis=0, concat_axis...]
  transfers between devices with their start and end apart: 6 -> 8, of which waited for: 5 -> 5; matrix products, arithmetic and copies ran while one was open for 6% -> 11% of each run, Pallas kernels for 0% -> 0%
where the time goes in v1:
time: 223 us; the launch traced here: 222 us
  waiting for transfers between devices  93.9 us (42%)
  blocking collectives  36.9 us (17%)
  other arithmetic  26.7 us (12%)
  local copies, waits for them, and re-layouts  20.4 us (9%)
  starting transfers between devices  18.3 us (8%)
  between operations  15.8 us (7%)
  matrix products  10.2 us (5%)
    psum x1, waiting for transfers between devices, local(): total = lax.psum(term, 'dom')  60.7 us
    ppermute x3, waiting for transfers between devices, resolve_block(): local_next = jax.lax.ppermute(local_next, mesh_dim, perm=new)  28.8 us
    all_to_all x1, blocking collectives, local(): lax.all_to_all(edge_side(recv_rows), 'dom', split_axis=0, concat_axis=0,...  10.2 us
    all_to_all x1, blocking collectives, local(): lax.all_to_all(grad_message.reshape(owners, -1, cols), 'dom', split_axis=...  9.74 us
    all_to_all x1, blocking collectives, local(): lax.all_to_all(edge_side(grad_recv), 'dom', split_axis=0, concat_axis=0,...  9.74 us
    unnamed x19, local copies, waits for them, and re-layouts  8.2 us
    all_gather x1, blocking collectives, local(): theta_full = lax.all_gather(theta, 'feat', axis=1, tiled=True)  7.21 us
    scatter-add x2, other arithmetic, vertex_side(): return dvis[:, None] * jax.ops.segment_sum(terms, vert, num_segments=nvert)  6.73 us
  transfers between devices with their start and end apart: 8, of which 5 were waited for; matrix products, arithmetic and copies ran while one was open for 11% of the time, Pallas kernels for 0%

profile of v1, /device:TPU:0, one launch (start us, length us, event | category | flops | bytes accessed | tf_op | source)
XLA Modules:
  0.0 222.2 jit_solution(14855904490598519930)
XLA Ops:
  8.5 14.6 %collective-permute-done = bf16[4096,128]{1,0:T(8,128)(2,1)S(1)} collective-permute-done((bf16[4096,128]{1,0:T(8,128)(2,1)}, bf16[4096,128]{1,0:T(8,128)(2,1)S(1)}, u32[]{:S(2)}, u32[]{:S(2)}) %collective-permute-start) | collective-permute-done | bytes 1048608 | tf_op jit(solution)/shard_map/ppermute | solution.py:15
  23.2 14.2 %collective-permute-done.1 = bf16[4096,128]{1,0:T(8,128)(2,1)S(1)} collective-permute-done((bf16[4096,128]{1,0:T(8,128)(2,1)S(1)}, bf16[4096,128]{1,0:T(8,128)(2,1)S(1)}, u32[]{:S(2)}, u32[]{:S(2)}) %collective-permute-start.1) | collective-permute-done | bytes 1048608 | tf_op jit(solution)/shard_map/ppermute | solution.py:15
  38.9 6.6 %all-to-all-start = ((s32[8,1,64]{2,1,0:T(1,128)}), s32[8,1,64]{2,1,0:T(1,128)S(1)}, u32[]{:S(2)}, u32[]{:S(2)}) async-start(s32[8,1,64]{2,1,0:T(1,128)} %all_to_all.24), calls=%async_computation | async-start | bytes 8192 | tf_op jit(solution)/shard_map/all_to_all | solution.py:38
  46.9 3.3 %scatter_custom_fusion = f32[4096]{0:T(1024)S(1)} fusion(s32[512]{0:T(512)S(1)} %bitcast.37, f32[512]{0:T(512)S(1)} %bitcast.32, f32[]{:T(128)} %constant.16.clone.1), kind=kCustom, calls=%fused_computation.50 | custom fusion | flops 512 | bytes 16388 | tf_op jit(solution)/shard_map/scatter-add | solution.py:29
  51.9 5.1 %all-to-all-start.1 = ((s32[8,1,64]{2,1,0:T(1,128)}), s32[8,1,64]{2,1,0:T(1,128)S(1)}, u32[]{:S(2)}, u32[]{:S(2)}) async-start(s32[8,1,64]{2,1,0:T(1,128)} %all_to_all.26), calls=%async_computation.1 | async-start | bytes 8192 | tf_op jit(solution)/shard_map/all_to_all | solution.py:39
  57.1 3.1 %gather_fusion = f32[512]{0:T(512)S(1)} fusion(f32[4096]{0:T(1024)S(1)} %rsqrt.3, s32[1024]{0:T(1024)S(1)} %get-tuple-element.10), kind=kCustom, calls=%fused_computation | custom fusion | bytes 6144 | tf_op jit(solution)/shard_map/gather | solution.py:30
  60.3 1.5 constant_dynamic-update-slice_fusion.7
  63.0 1.6 constant_dynamic-update-slice_fusion.3
  65.7 3.2 %copy-done.2 = bf16[4096,1024]{1,0:T(8,128)(2,1)} copy-done((bf16[4096,1024]{1,0:T(8,128)(2,1)}, bf16[4096,1024]{1,0:T(8,128)(2,1)S(1)}, u32[]{:S(2)}) %copy-start.2) | copy-done | bytes 8388632
  72.4 6.0 %all-to-all-start.2 = ((bf16[8,64,128]{2,1,0:T(8,128)(2,1)}), bf16[8,64,128]{2,1,0:T(8,128)(2,1)S(1)}, u32[]{:S(2)}, u32[]{:S(2)}) async-start(bf16[8,64,128]{2,1,0:T(8,128)(2,1)} %fusion.13), calls=%async_computation.2 | async-start | bytes 262144 | tf_op jit(solution)/shard_map/all_to_all | solution.py:35
  79.7 3.3 %scatter_custom_fusion.1 = f32[2048]{0:T(1024)S(1)} fusion(s32[512]{0:T(512)S(1)} %reshape.181, f32[512]{0:T(512)S(1)} %reshape.183, f32[]{:T(128)} %constant.16.clone.1), kind=kCustom, calls=%fused_computation.55 | custom fusion | flops 512 | bytes 8196 | tf_op jit(solution)/shard_map/scatter-add | solution.py:42
  83.0 2.9 %all-to-all-done.2 = bf16[8,64,128]{2,1,0:T(8,128)(2,1)S(1)} async-done(((bf16[8,64,128]{2,1,0:T(8,128)(2,1)}), bf16[8,64,128]{2,1,0:T(8,128)(2,1)S(1)}, u32[]{:S(2)}, u32[]{:S(2)}) %all-to-all-start.2) | async-done | bytes 131104 | tf_op jit(solution)/shard_map/all_to_all | solution.py:35
  86.0 2.5 %scatter_custom_fusion.2 = f32[2048,128]{1,0:T(8,128)S(1)} fusion(s32[512]{0:T(512)S(1)} %reshape.181, f32[]{:T(128)} %constant.17.clone.1, bf16[512,128]{1,0:T(8,128)(2,1)S(1)} %bitcast.24), kind=kCustom, calls=%fused_computation.28 | custom fusion | flops 131072 | bytes 1179652 | tf_op jit(solution)/shard_map/scatter-add | solution.py:48
  90.2 10.2 %all_to_all.38 = bf16[8,64,128]{2,1,0:T(8,128)(2,1)S(1)} all-to-all(bf16[8,64,128]{2,1,0:T(8,128)(2,1)S(1)} %bitcast.29), channel_id=1, replica_groups=mesh['dom'=8,'feat'=4] {'dom'}, dimensions={0} | all-to-all | bytes 262144 | tf_op jit(solution)/shard_map/all_to_all | solution.py:58
  100.4 3.9 %scatter_custom_fusion.3 = f32[4096,128]{1,0:T(8,128)} fusion(s32[512]{0:T(512)S(1)} %bitcast.38, f32[]{:T(128)} %constant.17.clone.1, bf16[512,128]{1,0:T(8,128)(2,1)S(1)} %bitcast.30, f32[512]{0:T(512)S(1)} %bitcast.33), kind=kCustom, calls=%fused_computation.24 | custom fusion | flops 196608 | bytes 2230276 | tf_op jit(solution)/shard_map/scatter-add | solution.py:56
  104.2 3.1 %multiply_multiply_fusion = (f32[4096,128]{1,0:T(8,128)S(1)}, bf16[4096,128]{1,0:T(8,128)(2,1)}) fusion(bf16[4096,128]{1,0:T(8,128)(2,1)S(1)} %copy-done.3, f32[4096,128]{1,0:T(8,128)} %scatter_custom_fusion.3, f32[4096]{0:T(1024)S(1)} %rsqrt.3), kind=kLoop, calls=%fused_computation.17 | loop fusion | flops 6291456 | bytes 6307840 | tf_op jit(solution)/shard_map/mul | solution.py:63
  108.5 9.7 %all_to_all.39 = bf16[8,64,128]{2,1,0:T(8,128)(2,1)S(1)} all-to-all(bf16[8,64,128]{2,1,0:T(8,128)(2,1)S(1)} %multiply_convert_fusion.4), channel_id=1, replica_groups=mesh['dom'=8,'feat'=4] {'dom'}, dimensions={0} | all-to-all | bytes 262144 | tf_op jit(solution)/shard_map/all_to_all | solution.py:65
  118.3 2.5 %scatter_custom_fusion.4 = f32[2048,128]{1,0:T(8,128)S(1)} fusion(s32[512]{0:T(512)S(1)} %reshape.181, f32[]{:T(128)} %constant.17.clone.1, bf16[512,128]{1,0:T(8,128)(2,1)S(1)} %bitcast.26), kind=kCustom, calls=%fused_computation.26 | custom fusion | flops 131072 | bytes 1179652 | tf_op jit(solution)/shard_map/scatter-add | solution.py:48
  122.5 9.7 %all_to_all.40 = bf16[8,64,128]{2,1,0:T(8,128)(2,1)S(1)} all-to-all(bf16[8,64,128]{2,1,0:T(8,128)(2,1)S(1)} %bitcast.27), channel_id=1, replica_groups=mesh['dom'=8,'feat'=4] {'dom'}, dimensions={0} | all-to-all | bytes 262144 | tf_op jit(solution)/shard_map/all_to_all | solution.py:68
  132.2 2.9 %scatter_custom_fusion.5 = f32[4096,128]{1,0:T(8,128)S(1)} fusion(s32[512]{0:T(512)S(1)} %bitcast.39, f32[]{:T(128)} %constant.17.clone.1, bf16[512,128]{1,0:T(8,128)(2,1)S(1)} %bitcast.25, f32[512]{0:T(512)S(1)} %bitcast.34), kind=kCustom, calls=%fused_computation.22 | custom fusion | flops 196608 | bytes 2230276 | tf_op jit(solution)/shard_map/scatter-add | solution.py:56
  135.9 4.6 %fusion = f32[512,128]{1,0:T(8,128)} fusion(bf16[4096,128]{1,0:T(8,128)(2,1)S(1)} %multiply_convert_fusion, bf16[4096,1024]{1,0:T(8,128)(2,1)} %copy-done.2, s32[]{:T(128)S(6)} %select_n.44), kind=kOutput, calls=%fused_computation.13 | convolution fusion | flops 536870912 | bytes 5505028 | tf_op jit(solution)/shard_map/dot_general | solution.py:80
  141.0 7.2 %all_gather.7 = bf16[512,512]{1,0:T(8,128)(2,1)S(1)} all-gather(bf16[512,128]{1,0:T(8,128)(2,1)S(1)} %copy-done.4), channel_id=1, replica_groups=mesh['dom'=8,'feat'=4] {'feat'}, dimensions={1}, use_global_device_ids=true | all-gather | bytes 655360 | tf_op jit(solution)/shard_map/all_gather | solution.py:70
  148.2 60.7 %all-reduce.2.cloned.1.call-done = f32[512,128]{1,0:T(8,128)} async-done(((f32[512,128]{1,0:T(8,128)}), f32[512,128]{1,0:T(8,128)}) %all-reduce.2.cloned.1.call-update) | async-done | bytes 262160 | tf_op jit(solution)/shard_map/psum | solution.py:83
  210.3 4.4 %convolution_convert_fusion = bf16[4096,128]{1,0:T(8,128)(2,1)} fusion(bf16[4096,512]{1,0:T(8,128)(2,1)} %all-gather.2.cloned.1.call-done, bf16[512,512]{1,0:T(8,128)(2,1)S(1)} %all_gather.7, s32[]{:T(128)S(6)} %select_n.46), kind=kOutput, calls=%fused_computation.11 | convolution fusion | flops 537395200 | bytes 5373956 | tf_op jit(solution)/shard_map/dot_general | solution.py:72
  (57 shorter events, 19.5 us)
Async XLA Ops:
  8.0 15.1 %collective-permute-start = (bf16[4096,128]{1,0:T(8,128)(2,1)}, bf16[4096,128]{1,0:T(8,128)(2,1)S(1)}, u32[]{:S(2)}, u32[]{:S(2)}) collective-permute-start(bf16[4096,128]{1,0:T(8,128)(2,1)} %param.5), channel_id=1, source_target_pairs={{0,1},{1,2},{2,3},{3,0},{4,5},{5,6},{6,7},{7,4},{8,9},{9,10},{10,1... | collective-permute-start | bytes 3145736 | tf_op jit(solution)/shard_map/ppermute | solution.py:15
  23.1 14.2 %collective-permute-start.1 = (bf16[4096,128]{1,0:T(8,128)(2,1)S(1)}, bf16[4096,128]{1,0:T(8,128)(2,1)S(1)}, u32[]{:S(2)}, u32[]{:S(2)}) collective-permute-start(bf16[4096,128]{1,0:T(8,128)(2,1)S(1)} %collective-permute-done), channel_id=1, source_target_pairs={{0,1},{1,2},{2,3},{3,0},{4,5},{5,6},{6,7},{7,4},{8,9},{9,10},{10,1... | collective-permute-start | bytes 3145736 | tf_op jit(solution)/shard_map/ppermute | solution.py:15
  37.3 23.0 %collective-permute-start.2 = (bf16[4096,128]{1,0:T(8,128)(2,1)S(1)}, bf16[4096,128]{1,0:T(8,128)(2,1)}, u32[]{:S(2)}, u32[]{:S(2)}) collective-permute-start(bf16[4096,128]{1,0:T(8,128)(2,1)S(1)} %collective-permute-done.1), channel_id=1, source_target_pairs={{0,1},{1,2},{2,3},{3,0},{4,5},{5,6},{6,7},{7,4},{8,9},{9,10},{10,1... | collective-permute-start | bytes 3145736 | tf_op jit(solution)/shard_map/ppermute | solution.py:15
  38.9 13.0 %all-to-all-start = ((s32[8,1,64]{2,1,0:T(1,128)}), s32[8,1,64]{2,1,0:T(1,128)S(1)}, u32[]{:S(2)}, u32[]{:S(2)}) async-start(s32[8,1,64]{2,1,0:T(1,128)} %all_to_all.24), calls=%async_computation | async-start | bytes 8192 | tf_op jit(solution)/shard_map/all_to_all | solution.py:38
  51.9 20.5 %all-to-all-start.1 = ((s32[8,1,64]{2,1,0:T(1,128)}), s32[8,1,64]{2,1,0:T(1,128)S(1)}, u32[]{:S(2)}, u32[]{:S(2)}) async-start(s32[8,1,64]{2,1,0:T(1,128)} %all_to_all.26), calls=%async_computation.1 | async-start | bytes 8192 | tf_op jit(solution)/shard_map/all_to_all | solution.py:39
  57.1 5.5 %copy-start.1 = (bf16[4096,128]{1,0:T(8,128)(2,1)S(1)}, bf16[4096,128]{1,0:T(8,128)(2,1)}, u32[]{:S(2)}) copy-start(bf16[4096,128]{1,0:T(8,128)(2,1)} %param.5) | copy-start | bytes 3145732
  63.0 6.0 %copy-start.4 = (bf16[512,128]{1,0:T(8,128)(2,1)S(1)}, bf16[512,128]{1,0:T(8,128)(2,1)}, u32[]{:S(2)}) copy-start(bf16[512,128]{1,0:T(8,128)(2,1)} %param.6) | copy-start | bytes 393220
  65.7 3.2 %copy-start.2 = (bf16[4096,1024]{1,0:T(8,128)(2,1)}, bf16[4096,1024]{1,0:T(8,128)(2,1)S(1)}, u32[]{:S(2)}) copy-start(bf16[4096,1024]{1,0:T(8,128)(2,1)S(1)} %constant_dynamic-update-slice_fusion) | copy-start | bytes 25165828
  68.9 14.1 %copy-start.5 = (f32[2048]{0:T(1024)S(1)}, f32[2048]{0:T(1024)}, u32[]{:S(2)}) copy-start(f32[2048]{0:T(1024)} %param.8) | copy-start | bytes 24580
  70.2 34.0 %copy-start.3 = (bf16[4096,128]{1,0:T(8,128)(2,1)S(1)}, bf16[4096,128]{1,0:T(8,128)(2,1)}, u32[]{:S(2)}) copy-start(bf16[4096,128]{1,0:T(8,128)(2,1)} %param.9) | copy-start | bytes 3145732
  72.4 13.6 %all-to-all-start.2 = ((bf16[8,64,128]{2,1,0:T(8,128)(2,1)}), bf16[8,64,128]{2,1,0:T(8,128)(2,1)S(1)}, u32[]{:S(2)}, u32[]{:S(2)}) async-start(bf16[8,64,128]{2,1,0:T(8,128)(2,1)} %fusion.13), calls=%async_computation.2 | async-start | bytes 262144 | tf_op jit(solution)/shard_map/all_to_all | solution.py:35
  78.4 130.6 %all-reduce.2.cloned.1.call-start = ((), (), s32[]{:S(2)}) async-start(), calls=%async_computation.7 | async-start | bytes 524288 | tf_op jit(solution)/shard_map/psum | solution.py:83
  135.8 4.7 %copy-start = (bf16[4096,128]{1,0:T(8,128)(2,1)}, bf16[4096,128]{1,0:T(8,128)(2,1)S(1)}, u32[]{:S(2)}) copy-start(bf16[4096,128]{1,0:T(8,128)(2,1)S(1)} %multiply_convert_fusion) | copy-start | bytes 3145732
  140.4 69.9 %all-gather.2.cloned.1.call-start = ((), (), s32[]{:S(2)}) async-start(), calls=%async_computation.6 | async-start | bytes 5242880 | tf_op jit(solution)/shard_map/all_gather | solution.py:73
Sparse Core Ops, SparseCore 0:
  140.6 68.3 all-reduce.1
Sparse Core Ops, SparseCore 1:
  143.0 32.7 all-gather.1
